TPU v7x, 32 devices: a whole 2x2x4 slice. The times are simulated.
32 devices in a mesh: seq: 8 (over z, x), rep: 4 (over y, core).
Axes of the slice: x: 2, y: 2, z: 4, core: 2. Of those that a mesh axis runs over, the one named last changes fastest.
Arguments:
- queries: bfloat16 [4096, 8192], P(('rep', 'seq')), may hold values from -6 to 6
- keys: bfloat16 [4096, 1024], P(('rep', 'seq')), may hold values from -6 to 6
- values: bfloat16 [4096, 1024], P(('rep', 'seq')), may hold values from -6 to 6
- vertical: int32 [64, 24], replicated, may hold values from -1 to 63, as said below
- slash: int32 [64, 24], replicated, may hold values from -1 to 63, as said below
Outputs:
- attention: bfloat16 [4096, 8192], P(('rep', 'seq'))
Inputs may be any that keep to these rules, and one draw needn't show every extreme that they name: `vertical`: in each row the entries other than -1 come first and are distinct; every row has at least one; some row has all 24 in use. `slash`: each row begins with 0; the entries other than -1 come first and are distinct; some row has all 24 in use.
All inputs are finite; a program needn't handle non-finite values.
Results may differ from a plain program's by a relative error of at most 0.0055.
Values may be sent and summed in bfloat16 or wider, within the bound.
A program may use at most 128 MiB of HBM per device.

v0:
```python
import functools
import math

import jax
import jax.numpy as jnp
from jax import lax
from jax.experimental import pallas as pl
from jax.experimental.pallas import tpu as pltpu
from jax.sharding import PartitionSpec as P

QUERY_HEADS = 64
KEY_VALUE_HEADS = 8
HEAD_SIZE = 128
BLOCK = 64
GROUP = QUERY_HEADS // KEY_VALUE_HEADS

MASKED = -1e30
KEY_TILE = 1024
ROW_TILE = 256
EXP2_SCALE = math.log2(math.e) / math.sqrt(HEAD_SIZE)


def attend_kernel(first_head, rows, position_ref, q_ref, k_ref, v_ref, mask_ref, own_mask_ref, *rest):
    out_ref, query_s, best_s, acc_s = rest[-4:]
    blocks = rows // BLOCK
    position = position_ref[0]
    head_base = (first_head + pl.program_id(0)) * GROUP
    lane = lax.broadcasted_iota(jnp.int32, (rows, HEAD_SIZE), 1)
    row_block = lax.broadcasted_iota(jnp.int32, (rows, HEAD_SIZE), 0) // BLOCK
    for head in range(GROUP):
        pick = lane == (head_base + head) * blocks + row_block
        query_s[head * rows : (head + 1) * rows, :HEAD_SIZE] = q_ref[
            :, head * HEAD_SIZE : (head + 1) * HEAD_SIZE
        ]
        query_s[head * rows : (head + 1) * rows, HEAD_SIZE:] = pick.astype(jnp.bfloat16)

    row_tile = min(ROW_TILE, GROUP * rows)
    tiles = [slice(i, i + row_tile) for i in range(0, GROUP * rows, row_tile)]
    contract = (((1,), (1,)), ((), ()))

    own = pl.ds(pl.multiple_of(position * rows, rows), rows)
    own_keys = jnp.concatenate([k_ref[own, :], own_mask_ref[...]], axis=1)
    own_values = jnp.concatenate([v_ref[own, :], jnp.ones((rows, HEAD_SIZE), jnp.bfloat16)], axis=1)
    own_row = lax.broadcasted_iota(jnp.int32, (row_tile, rows), 0) % rows
    own_column = lax.broadcasted_iota(jnp.int32, (row_tile, rows), 1)
    for tile in tiles:
        scores = lax.dot_general(
            query_s[tile, :], own_keys, contract, preferred_element_type=jnp.float32
        )
        scores = jnp.where(own_column <= own_row, scores, MASKED)
        best = jnp.max(scores, axis=1, keepdims=True)
        weights = jnp.exp2((scores - best) * EXP2_SCALE).astype(jnp.bfloat16)
        best_s[tile, :] = jnp.broadcast_to(best, (row_tile, HEAD_SIZE))
        acc_s[tile, :] = jnp.dot(weights, own_values, preferred_element_type=jnp.float32)

    def key_step(step, _):
        here = pl.ds(pl.multiple_of(step * KEY_TILE, KEY_TILE), KEY_TILE)
        keys = jnp.concatenate([k_ref[here, :], mask_ref[here, :]], axis=1)
        values = jnp.concatenate(
            [v_ref[here, :], jnp.ones((KEY_TILE, HEAD_SIZE), jnp.bfloat16)], axis=1
        )
        for tile in tiles:
            scores = lax.dot_general(
                query_s[tile, :], keys, contract, preferred_element_type=jnp.float32
            )
            before = best_s[tile, :1]
            best = jnp.maximum(before, jnp.max(scores, axis=1, keepdims=True))
            factor = jnp.exp2((before - best) * EXP2_SCALE)
            weights = jnp.exp2((scores - best) * EXP2_SCALE).astype(jnp.bfloat16)
            best_s[tile, :] = jnp.broadcast_to(best, (row_tile, HEAD_SIZE))
            acc_s[tile, :] = acc_s[tile, :] * factor + jnp.dot(
                weights, values, preferred_element_type=jnp.float32
            )
        return 0

    lax.fori_loop(0, (position * rows + KEY_TILE - 1) // KEY_TILE, key_step, 0)

    for head in range(GROUP):
        tile = slice(head * rows, (head + 1) * rows)
        out_ref[:, head * HEAD_SIZE : (head + 1) * HEAD_SIZE] = (
            acc_s[tile, :HEAD_SIZE] / acc_s[tile, HEAD_SIZE:]
        ).astype(jnp.bfloat16)


def attend(position, queries, gathered, mask, own_mask, out, first_head, heads):
    rows = queries.shape[0]
    tokens = gathered.shape[0]
    once = pl.Buffered(1)
    in_specs = [
        pl.BlockSpec((rows, GROUP * HEAD_SIZE), lambda g, s: (0, first_head + g)),
        pl.BlockSpec((tokens, HEAD_SIZE), lambda g, s: (0, g)),
        pl.BlockSpec((tokens, HEAD_SIZE), lambda g, s: (0, heads + g)),
        pl.BlockSpec((tokens, HEAD_SIZE), lambda g, s: (0, 0), pipeline_mode=once),
        pl.BlockSpec((rows, HEAD_SIZE), lambda g, s: (0, 0), pipeline_mode=once),
    ]
    operands = [position, queries, gathered, gathered, mask, own_mask]
    aliases = {}
    if out is not None:
        in_specs.append(pl.BlockSpec(memory_space=pl.ANY))
        aliases = {len(operands): 0}
        operands.append(out)
    pairs = heads * GROUP * rows * tokens
    return pl.pallas_call(
        functools.partial(attend_kernel, first_head, rows),
        out_shape=jax.ShapeDtypeStruct(queries.shape, jnp.bfloat16),
        grid_spec=pltpu.PrefetchScalarGridSpec(
            num_scalar_prefetch=1,
            grid=(heads,),
            in_specs=in_specs,
            out_specs=pl.BlockSpec((rows, GROUP * HEAD_SIZE), lambda g, s: (0, first_head + g)),
            scratch_shapes=[
                pltpu.VMEM((GROUP * rows, 2 * HEAD_SIZE), jnp.bfloat16),
                pltpu.VMEM((GROUP * rows, HEAD_SIZE), jnp.float32),
                pltpu.VMEM((GROUP * rows, 2 * HEAD_SIZE), jnp.float32),
            ],
        ),
        input_output_aliases=aliases,
        compiler_params=pltpu.CompilerParams(
            vmem_limit_bytes=60 << 20
        ),
        cost_estimate=pl.CostEstimate(
            flops=pairs * HEAD_SIZE * 8,
            bytes_accessed=heads * tokens * HEAD_SIZE * 4,
            transcendentals=pairs,
        ),
    )(*operands)


def mask_columns(vertical, slash, first_block, blocks, block_total):
    key_block = jnp.arange(block_total, dtype=jnp.int32)
    here = first_block + jnp.arange(blocks, dtype=jnp.int32)
    column = jnp.any(vertical[None] == key_block[:, None, None], axis=-1)
    gap = here[None, :] - key_block[:, None]
    diagonal = jnp.any(slash[None, :, None, :] == gap[:, None, :, None], axis=-1)
    allowed = column[:, :, None] | diagonal
    earlier = (key_block < first_block)[:, None, None]
    width = QUERY_HEADS * blocks

    def spread(keep):
        fill = jnp.where(keep, 0.0, MASKED).astype(jnp.bfloat16).reshape(-1, width)
        return jnp.repeat(fill, BLOCK, axis=0)

    own = lax.dynamic_slice_in_dim(allowed, first_block, blocks, 0)
    return spread(allowed & earlier), spread(own)


def body(queries, keys, values, vertical, slash):
    rows = queries.shape[0]
    ways = lax.axis_size("rep") * lax.axis_size("seq")
    tokens = rows * ways
    position = lax.axis_index("rep") * lax.axis_size("seq") + lax.axis_index("seq")
    total_bytes = 2 * tokens * keys.shape[1] * keys.dtype.itemsize
    tight = total_bytes > (32 << 20)
    heads = 1 if tight else 2
    mask, own_mask = mask_columns(
        vertical, slash, position * (rows // BLOCK), rows // BLOCK, tokens // BLOCK
    )
    position = position.astype(jnp.int32).reshape(1)
    out = None
    for first in range(0, KEY_VALUE_HEADS, heads):
        columns = slice(first * HEAD_SIZE, (first + heads) * HEAD_SIZE)
        part = jnp.concatenate([keys[:, columns], values[:, columns]], axis=1)
        if tight and out is not None:
            part, out = lax.optimization_barrier((part, out))
        gathered = lax.all_gather(part, ("rep", "seq"), axis=0, tiled=True)
        out = attend(position, queries, gathered, mask, own_mask, out, first, heads)
    return out


def solution(mesh):
    in_specs = (P(("rep", "seq"), None), P(("rep", "seq"), None), P(("rep", "seq"), None), P(), P())
    out_specs = P(("rep", "seq"), None)
    return jax.shard_map(body, mesh=mesh, in_specs=in_specs, out_specs=out_specs, check_vma=False)
```

profile of v0, /device:TPU:13, one launch (start us, length us, event | category | flops | bytes accessed | tf_op | source)
XLA Modules:
  0.0 291.7 jit_solution(15312590835462671411)
XLA Ops:
  6.5 1.1 fusion.2
  7.7 0.7 pad_maximum_fusion.3
  8.4 0.7 pad_maximum_fusion.2
  9.1 0.0 all-gather.7.cloned.1.call-start
  9.2 0.7 pad_maximum_fusion.1
  9.9 0.7 pad_maximum_fusion
  10.6 0.2 fusion
  10.8 0.5 compare_reduce_fusion
  11.3 0.1 broadcast_or_fusion
  11.4 0.1 copy.18
  11.5 0.1 copy.20
  11.6 0.1 reshape.47
  11.8 0.1 copy.19
  11.9 0.1 select_convert_fusion
  12.0 61.9 %all-gather.11.cloned.1.call-done.k_ref.v_ref = bf16[4096,512]{1,0:T(8,128)(2,1)} async-done(((bf16[128,512]{1,0:T(8,128)(2,1)}), bf16[4096,512]{1,0:T(8,128)(2,1)}) %all-gather.11.cloned.1.call-update) | async-done | bytes 4194320 | tf_op jit(solution)/shard_map/all_gather | solution.py:165
  74.0 0.6 broadcast_in_dim.35
  74.6 1.1 broadcast_in_dim.32
  75.7 20.3 %shard_map.55.rest_0_ = bf16[128,8192]{1,0:T(8,128)(2,1)} custom-call(s32[1]{0:T(128)} %bitcast.position_ref, bf16[128,8192]{1,0:T(8,128)(2,1)} %q_ref.7, bf16[4096,512]{1,0:T(8,128)(2,1)} %all-gather.11.cloned.1.call-done.k_ref.v_ref, bf16[4096,512]{1,0:T(8,128)(2,1)} %all-gather.11.cloned.1.call-done.k_ref.v_ref, bf16[4096,128]{1,0:T(8,128)(2,1)} %bitcast.5, ...), custom_call_target="tpu_custom_call" | custom-call | flops 8589934592 | bytes 4194304 | tf_op jit(solution)/shard_map/pallas_call | solution.py:103
  96.0 41.7 %all-gather.9.cloned.1.call-done.k_ref.v_ref = bf16[4096,512]{1,0:T(8,128)(2,1)} async-done(((bf16[128,512]{1,0:T(8,128)(2,1)}), bf16[4096,512]{1,0:T(8,128)(2,1)}) %all-gather.9.cloned.1.call-update) | async-done | bytes 4194320 | tf_op jit(solution)/shard_map/all_gather | solution.py:165
  137.7 20.3 %shard_map.56.rest_0_ = bf16[128,8192]{1,0:T(8,128)(2,1)} custom-call(s32[1]{0:T(128)} %bitcast.position_ref, bf16[128,8192]{1,0:T(8,128)(2,1)} %q_ref.7, bf16[4096,512]{1,0:T(8,128)(2,1)} %all-gather.9.cloned.1.call-done.k_ref.v_ref, bf16[4096,512]{1,0:T(8,128)(2,1)} %all-gather.9.cloned.1.call-done.k_ref.v_ref, ...), custom_call_target="tpu_custom_call", output_to_operand_aliasing={{}: (6, {})} | custom-call | flops 8589934592 | bytes 4194304 | tf_op jit(solution)/shard_map/pallas_call | solution.py:103
  157.9 43.4 %all-gather.7.cloned.1.call-done.k_ref.v_ref = bf16[4096,512]{1,0:T(8,128)(2,1)} async-done(((bf16[128,512]{1,0:T(8,128)(2,1)}), bf16[4096,512]{1,0:T(8,128)(2,1)}) %all-gather.7.cloned.1.call-update) | async-done | bytes 4194320 | tf_op jit(solution)/shard_map/all_gather | solution.py:165
  201.3 20.3 %shard_map.57.rest_0_ = bf16[128,8192]{1,0:T(8,128)(2,1)} custom-call(s32[1]{0:T(128)} %bitcast.position_ref, bf16[128,8192]{1,0:T(8,128)(2,1)} %q_ref.7, bf16[4096,512]{1,0:T(8,128)(2,1)} %all-gather.7.cloned.1.call-done.k_ref.v_ref, bf16[4096,512]{1,0:T(8,128)(2,1)} %all-gather.7.cloned.1.call-done.k_ref.v_ref, ...), custom_call_target="tpu_custom_call", output_to_operand_aliasing={{}: (6, {})} | custom-call | flops 8589934592 | bytes 4194304 | tf_op jit(solution)/shard_map/pallas_call | solution.py:103
  221.6 43.3 %all-gather.5.cloned.1.call-done.k_ref.v_ref = bf16[4096,512]{1,0:T(8,128)(2,1)} async-done(((bf16[128,512]{1,0:T(8,128)(2,1)}), bf16[4096,512]{1,0:T(8,128)(2,1)}) %all-gather.5.cloned.1.call-update) | async-done | bytes 4194320 | tf_op jit(solution)/shard_map/all_gather | solution.py:165
  264.9 20.3 %shard_map.58 = bf16[128,8192]{1,0:T(8,128)(2,1)} custom-call(s32[1]{0:T(128)} %bitcast.position_ref, bf16[128,8192]{1,0:T(8,128)(2,1)} %q_ref.7, bf16[4096,512]{1,0:T(8,128)(2,1)} %all-gather.5.cloned.1.call-done.k_ref.v_ref, bf16[4096,512]{1,0:T(8,128)(2,1)} %all-gather.5.cloned.1.call-done.k_ref.v_ref, ...), custom_call_target="tpu_custom_call", output_to_operand_aliasing={{}: (6, {})} | custom-call | flops 8589934592 | bytes 4194304 | tf_op jit(solution)/shard_map/pallas_call | solution.py:103
  (16 shorter events, 0.3 us)
Async XLA Ops:
  6.5 4.1 %copy-start.1 = (s32[64,24]{0,1:T(8,128)S(1)}, s32[64,24]{0,1:T(8,128)}, u32[]{:S(2)}) copy-start(s32[64,24]{0,1:T(8,128)} %param.8) | copy-start | bytes 18436
  6.5 4.3 %copy-start = (s32[64,24]{0,1:T(8,128)S(1)}, s32[64,24]{0,1:T(8,128)}, u32[]{:S(2)}) copy-start(s32[64,24]{0,1:T(8,128)} %param.9) | copy-start | bytes 18436
  6.5 67.4 %all-gather.11.cloned.1.call-start = ((), (), s32[]{:S(2)}) async-start(), calls=%async_computation.3 | async-start | bytes 4325376 | tf_op jit(solution)/shard_map/all_gather | solution.py:165
  8.4 129.3 %all-gather.9.cloned.1.call-start = ((), (), s32[]{:S(2)}) async-start(), calls=%async_computation.2 | async-start | bytes 4325376 | tf_op jit(solution)/shard_map/all_gather | solution.py:165
  9.1 192.2 %all-gather.7.cloned.1.call-start = ((), (), s32[]{:S(2)}) async-start(), calls=%async_computation.1 | async-start | bytes 4325376 | tf_op jit(solution)/shard_map/all_gather | solution.py:165
  9.9 255.1 %all-gather.5.cloned.1.call-start = ((), (), s32[]{:S(2)}) async-start(), calls=%async_computation | async-start | bytes 4325376 | tf_op jit(solution)/shard_map/all_gather | solution.py:165
Sparse Core Ops, SparseCore 0:
  10.4 63.5 all-gather.10
  77.0 60.6 all-gather.8
  140.7 60.6 all-gather.6
  204.2 60.6 all-gather.4
where the time goes:
time: 292 us
  waiting for transfers between devices  190 us (65%)
  Pallas kernels  81.1 us (28%)
  between operations  13.2 us (5%)
  other arithmetic  3.46 us (1%)
  local copies, waits for them, and re-layouts  3.38 us (1%)
    all_gather x4, waiting for transfers between devices, body(): gathered = lax.all_gather(part, ('rep', 'seq'), axis=0, tiled=True)  190 us
    pallas_call x4, Pallas kernels, attend(): pl.pallas_call(functools.partial(attend_kernel, first_head, rows), out_sh...  81.1 us
  transfers between devices with their start and end apart: 4, of which 4 were waited for; matrix products, arithmetic and copies ran while one was open for 2% of the time, Pallas kernels for 21%

commit v1 on v0

--- a/solution.py
+++ b/solution.py
@@ -126,6 +126,198 @@
     )(*operands)
 
 
+def fused_kernel(
+    chunk, q_ref, key_ref, value_ref, mask_ref, own_mask_ref, out_ref,
+    pool, query_s, best_s, acc_s, send_sem, recv_sem,
+):
+    rows = key_ref.shape[0]
+    depth = pool.shape[4]
+    blocks = rows // BLOCK
+    seq, rep = lax.axis_index("seq"), lax.axis_index("rep")
+    z, x, y, core = seq // 2, seq % 2, rep // 2, rep % 2
+    z_peers = [((z + k) % depth) * 2 + x for k in range(1, depth)]
+    along_x = {"seq": z * 2 + 1 - x, "rep": rep}
+    along_y = {"seq": seq, "rep": (1 - y) * 2 + core}
+    sibling = {"seq": seq, "rep": y * 2 + 1 - core}
+    peers = [{"seq": peer, "rep": rep} for peer in z_peers] + [along_x, along_y, sibling]
+
+    for head in range(KEY_VALUE_HEADS):
+        columns = slice(head * HEAD_SIZE, (head + 1) * HEAD_SIZE)
+        pool[0, head, y, core, z, x] = key_ref[:, columns]
+        pool[1, head, y, core, z, x] = value_ref[:, columns]
+
+    barrier = pltpu.get_barrier_semaphore()
+    for peer in peers:
+        pl.semaphore_signal(
+            barrier, inc=1, device_id=peer, device_id_type=pl.DeviceIdType.MESH
+        )
+    pl.semaphore_wait(barrier, len(peers))
+
+    copies = {}
+
+    def send(kind, part, slot, ref, peer):
+        copy = pltpu.make_async_remote_copy(
+            src_ref=ref,
+            dst_ref=ref,
+            send_sem=send_sem.at[kind, part, slot],
+            recv_sem=recv_sem.at[kind, part, slot],
+            device_id=peer,
+            device_id_type=pl.DeviceIdType.MESH,
+        )
+        copy.start()
+        copies[kind, part, slot] = copy
+
+    def heads_of(part):
+        return pl.ds(part * chunk, chunk)
+
+    def stage_line(part):
+        for kind in range(2):
+            for k in range(depth - 1):
+                send(kind, part, k, pool.at[kind, heads_of(part), y, core, z, x], peers[k])
+
+    def stage_first(part):
+        for kind in range(2):
+            for k in range(depth - 1):
+                copies[kind, part, k].wait_recv()
+            send(
+                kind, part, depth - 1, pool.at[kind, heads_of(part), y, core, :, x],
+                along_y if kind else along_x,
+            )
+
+    def stage_second(part):
+        for kind in range(2):
+            copies[kind, part, depth - 1].wait_recv()
+        send(0, part, depth, pool.at[0, heads_of(part), y, core], along_y)
+        send(1, part, depth, pool.at[1, heads_of(part), :, core, :, x], along_x)
+
+    def stage_core(part):
+        for kind in range(2):
+            copies[kind, part, depth].wait_recv()
+            send(kind, part, depth + 1, pool.at[kind, heads_of(part), :, core], sibling)
+
+    def stage_done(part):
+        for kind in range(2):
+            copies[kind, part, depth + 1].wait_recv()
+
+    key_tile = depth * 2 * rows
+    steps = rep + (seq + 2 * depth - 1) // (2 * depth)
+    row_tile = min(ROW_TILE, GROUP * rows)
+    tiles = [slice(i, i + row_tile) for i in range(0, GROUP * rows, row_tile)]
+    contract = (((1,), (1,)), ((), ()))
+
+    def attend_group(group):
+        lane = lax.broadcasted_iota(jnp.int32, (rows, HEAD_SIZE), 1)
+        row_block = lax.broadcasted_iota(jnp.int32, (rows, HEAD_SIZE), 0) // BLOCK
+        for local in range(GROUP):
+            head = group * GROUP + local
+            here = slice(local * rows, (local + 1) * rows)
+            query_s[here, :HEAD_SIZE] = q_ref[:, head * HEAD_SIZE : (head + 1) * HEAD_SIZE]
+            query_s[here, HEAD_SIZE:] = (lane == head * blocks + row_block).astype(jnp.bfloat16)
+
+        own_keys = jnp.concatenate([pool[0, group, y, core, z, x], own_mask_ref[...]], axis=1)
+        own_values = jnp.concatenate(
+            [pool[1, group, y, core, z, x], jnp.ones((rows, HEAD_SIZE), jnp.bfloat16)], axis=1
+        )
+        own_row = lax.broadcasted_iota(jnp.int32, (row_tile, rows), 0) % rows
+        own_column = lax.broadcasted_iota(jnp.int32, (row_tile, rows), 1)
+        for tile in tiles:
+            scores = lax.dot_general(
+                query_s[tile, :], own_keys, contract, preferred_element_type=jnp.float32
+            )
+            scores = jnp.where(own_column <= own_row, scores, MASKED)
+            best = jnp.max(scores, axis=1, keepdims=True)
+            weights = jnp.exp2((scores - best) * EXP2_SCALE).astype(jnp.bfloat16)
+            best_s[tile, :] = jnp.broadcast_to(best, (row_tile, HEAD_SIZE))
+            acc_s[tile, :] = jnp.dot(weights, own_values, preferred_element_type=jnp.float32)
+
+        def key_step(step, _):
+            here = pl.ds(pl.multiple_of(step * key_tile, key_tile), key_tile)
+            key_rows = pool[0, group, step // 2, step % 2].reshape(key_tile, HEAD_SIZE)
+            value_rows = pool[1, group, step // 2, step % 2].reshape(key_tile, HEAD_SIZE)
+            keys = jnp.concatenate([key_rows, mask_ref[here, :]], axis=1)
+            values = jnp.concatenate(
+                [value_rows, jnp.ones((key_tile, HEAD_SIZE), jnp.bfloat16)], axis=1
+            )
+            for tile in tiles:
+                scores = lax.dot_general(
+                    query_s[tile, :], keys, contract, preferred_element_type=jnp.float32
+                )
+                before = best_s[tile, :1]
+                best = jnp.maximum(before, jnp.max(scores, axis=1, keepdims=True))
+                factor = jnp.exp2((before - best) * EXP2_SCALE)
+                weights = jnp.exp2((scores - best) * EXP2_SCALE).astype(jnp.bfloat16)
+                best_s[tile, :] = jnp.broadcast_to(best, (row_tile, HEAD_SIZE))
+                acc_s[tile, :] = acc_s[tile, :] * factor + jnp.dot(
+                    weights, values, preferred_element_type=jnp.float32
+                )
+            return 0
+
+        lax.fori_loop(0, steps, key_step, 0)
+        for local in range(GROUP):
+            head = group * GROUP + local
+            tile = slice(local * rows, (local + 1) * rows)
+            out_ref[:, head * HEAD_SIZE : (head + 1) * HEAD_SIZE] = (
+                acc_s[tile, :HEAD_SIZE] / acc_s[tile, HEAD_SIZE:]
+            ).astype(jnp.bfloat16)
+
+    for part in range(4):
+        stage_line(part)
+    stage_first(0)
+    stage_second(0)
+    stage_first(1)
+    stage_core(0)
+    stage_done(0)
+    attend_group(0)
+    stage_first(2)
+    stage_second(1)
+    attend_group(1)
+    stage_first(3)
+    stage_core(1)
+    stage_second(2)
+    stage_done(1)
+    attend_group(2)
+    stage_second(3)
+    stage_core(2)
+    attend_group(3)
+    stage_core(3)
+    stage_done(2)
+    attend_group(4)
+    attend_group(5)
+    stage_done(3)
+    attend_group(6)
+    attend_group(7)
+    for copy in copies.values():
+        copy.wait_send()
+
+
+def fused(queries, keys, values, mask, own_mask, depth):
+    rows = queries.shape[0]
+    parts = 4
+    tokens = mask.shape[0]
+    pairs = QUERY_HEADS * rows * tokens
+    whole = pl.BlockSpec(memory_space=pltpu.VMEM)
+    return pl.pallas_call(
+        functools.partial(fused_kernel, KEY_VALUE_HEADS // parts),
+        out_shape=jax.ShapeDtypeStruct(queries.shape, jnp.bfloat16),
+        in_specs=[whole] * 5,
+        out_specs=whole,
+        scratch_shapes=[
+            pltpu.VMEM((2, KEY_VALUE_HEADS, 2, 2, depth, 2, rows, HEAD_SIZE), jnp.bfloat16),
+            pltpu.VMEM((GROUP * rows, 2 * HEAD_SIZE), jnp.bfloat16),
+            pltpu.VMEM((GROUP * rows, HEAD_SIZE), jnp.float32),
+            pltpu.VMEM((GROUP * rows, 2 * HEAD_SIZE), jnp.float32),
+            pltpu.SemaphoreType.DMA((2, parts, depth + 2)),
+            pltpu.SemaphoreType.DMA((2, parts, depth + 2)),
+        ],
+        compiler_params=pltpu.CompilerParams(
+            collective_id=0, has_side_effects=True, vmem_limit_bytes=56 << 20
+        ),
+        cost_estimate=pl.CostEstimate(
+            flops=pairs * HEAD_SIZE * 8, bytes_accessed=8 << 20, transcendentals=pairs
+        ),
+    )(queries, keys, values, mask, own_mask)
+
+
 def mask_columns(vertical, slash, first_block, blocks, block_total):
     key_block = jnp.arange(block_total, dtype=jnp.int32)
     here = first_block + jnp.arange(blocks, dtype=jnp.int32)
@@ -151,10 +343,12 @@
     position = lax.axis_index("rep") * lax.axis_size("seq") + lax.axis_index("seq")
     total_bytes = 2 * tokens * keys.shape[1] * keys.dtype.itemsize
     tight = total_bytes > (32 << 20)
-    heads = 1 if tight else 2
+    heads = 1
     mask, own_mask = mask_columns(
         vertical, slash, position * (rows // BLOCK), rows // BLOCK, tokens // BLOCK
     )
+    if not tight and lax.axis_size("rep") == 4 and lax.axis_size("seq") % 2 == 0:
+        return fused(queries, keys, values, mask, own_mask, lax.axis_size("seq") // 2)
     position = position.astype(jnp.int32).reshape(1)
     out = None
     for first in range(0, KEY_VALUE_HEADS, heads):

time: 292 us -> 144 us (0.49)
  waiting for transfers between devices: 190 us -> 0 us
  Pallas kernels: 81.1 us -> 136 us
  between operations: 13.2 us -> 0.07 us
    all_gather x4 -> x0, waiting for transfers between devices: 190 us -> none  [body(): gathered = lax.all_gather(part, ('rep', 'seq'), axis=0, tiled=True)]
    pallas_call x4 -> x1, Pallas kernels: 81.1 us -> 136 us  [fused(): pl.pallas_call(functools.partial(fused_kernel, KEY_VALUE_HEADS // parts),...]
    unnamed x4 -> x1, local copies, waits for them, and re-layouts: 0.01 us -> 3.1 us
  transfers between devices with their start and end apart: 4 -> 0, of which waited for: 4 -> 0; matrix products, arithmetic and copies ran while one was open for 2% -> 0% of each run, Pallas kernels for 21% -> 0%
where the time goes in v1:
time: 144 us
  Pallas kernels  136 us (94%)
  local copies, waits for them, and re-layouts  5.36 us (4%)
  other arithmetic  2.16 us (2%)
    pallas_call x1, Pallas kernels, fused(): pl.pallas_call(functools.partial(fused_kernel, KEY_VALUE_HEADS // parts),...  136 us
    unnamed x1, local copies, waits for them, and re-layouts  3.1 us

profile of v1, /device:TPU:13, one launch (start us, length us, event | category | flops | bytes accessed | tf_op | source)
XLA Modules:
  0.0 143.5 jit_solution(15846708130768134679)
XLA Ops:
  0.0 0.9 fusion
  0.9 1.1 compare_reduce_fusion
  2.0 0.1 broadcast_or_fusion
  2.1 0.1 copy.15
  2.3 0.1 copy.16
  2.4 0.1 select_convert_fusion
  2.5 0.1 copy.17
  2.6 0.2 reshape.43
  2.8 0.6 broadcast_in_dim.35
  3.4 1.1 broadcast_in_dim.32
  4.5 135.9 %shard_map.55 = bf16[128,8192]{1,0:T(8,128)(2,1)} custom-call(bf16[128,8192]{1,0:T(8,128)(2,1)} %q_ref.1, bf16[128,1024]{1,0:T(8,128)(2,1)} %key_ref.1, bf16[128,1024]{1,0:T(8,128)(2,1)} %value_ref.1, bf16[4096,128]{1,0:T(8,128)(2,1)} %bitcast.4, bf16[128,128]{1,0:T(8,128)(2,1)} %bitcast.5), custom_call_target="tpu_custom_call" | custom-call | flops 34359738368 | bytes 8388608 | tf_op jit(solution)/shard_map/pallas_call | solution.py:299
  140.4 3.1 %copy.19 = bf16[128,8192]{1,0:T(8,128)(2,1)} copy(bf16[128,8192]{1,0:T(8,128)(2,1)} %shard_map.55) | data formatting | bytes 4194304
  (5 shorter events, 0.1 us)

commit v2 on v1

--- a/solution.py
+++ b/solution.py
@@ -127,8 +127,8 @@
 
 
 def fused_kernel(
-    chunk, q_ref, key_ref, value_ref, mask_ref, own_mask_ref, out_ref,
-    pool, query_s, best_s, acc_s, send_sem, recv_sem,
+    q_ref, key_ref, value_ref, column_ref, offset_ref, out_ref,
+    pool, mask_ref, own_mask_ref, bias_s, query_s, best_s, acc_s, send_sem, recv_sem,
 ):
     rows = key_ref.shape[0]
     depth = pool.shape[4]
@@ -168,7 +168,7 @@
         copies[kind, part, slot] = copy
 
     def heads_of(part):
-        return pl.ds(part * chunk, chunk)
+        return part
 
     def stage_line(part):
         for kind in range(2):
@@ -201,18 +201,51 @@
 
     key_tile = depth * 2 * rows
     steps = rep + (seq + 2 * depth - 1) // (2 * depth)
-    row_tile = min(ROW_TILE, GROUP * rows)
-    tiles = [slice(i, i + row_tile) for i in range(0, GROUP * rows, row_tile)]
     contract = (((1,), (1,)), ((), ()))
 
-    def attend_group(group):
+    first_block = (rep * (2 * depth) + seq) * blocks
+
+    def allowed_blocks(key_block):
+        gap = first_block + lax.broadcasted_iota(jnp.int32, key_block.shape, 1) % blocks - key_block
+        allowed = (column_ref[:1, :] == key_block) | (offset_ref[:1, :] == gap)
+        for slot in range(1, column_ref.shape[0]):
+            allowed = allowed | (column_ref[slot : slot + 1, :] == key_block)
+        for slot in range(1, offset_ref.shape[0]):
+            allowed = allowed | (offset_ref[slot : slot + 1, :] == gap)
+        return allowed
+
+    def build_masks():
+        key_block = lax.broadcasted_iota(jnp.int32, bias_s.shape, 0)
+        keep = allowed_blocks(key_block) & (key_block < first_block)
+        bias_s[...] = jnp.where(keep, 0.0, MASKED)
+        for block in range(bias_s.shape[0]):
+            mask_ref[block * BLOCK : (block + 1) * BLOCK, :] = jnp.broadcast_to(
+                bias_s[block : block + 1, :], (BLOCK, HEAD_SIZE)
+            ).astype(jnp.bfloat16)
+        own_block = first_block + (
+            lax.broadcasted_iota(jnp.int32, own_mask_ref.shape, 0) // BLOCK
+        )
+        own_mask_ref[...] = jnp.where(allowed_blocks(own_block), 0.0, MASKED).astype(jnp.bfloat16)
+
+    def attend_heads(group, locals_here):
         lane = lax.broadcasted_iota(jnp.int32, (rows, HEAD_SIZE), 1)
         row_block = lax.broadcasted_iota(jnp.int32, (rows, HEAD_SIZE), 0) // BLOCK
-        for local in range(GROUP):
+        for place, local in enumerate(locals_here):
             head = group * GROUP + local
-            here = slice(local * rows, (local + 1) * rows)
+            here = slice(place * rows, (place + 1) * rows)
             query_s[here, :HEAD_SIZE] = q_ref[:, head * HEAD_SIZE : (head + 1) * HEAD_SIZE]
             query_s[here, HEAD_SIZE:] = (lane == head * blocks + row_block).astype(jnp.bfloat16)
+
+        row_tile = min(ROW_TILE, len(locals_here) * rows)
+        tiles = [slice(i, i + row_tile) for i in range(0, len(locals_here) * rows, row_tile)]
+
+        def logits(keys):
+            return [
+                lax.dot_general(
+                    query_s[tile, :], keys, contract, preferred_element_type=jnp.float32
+                )
+                for tile in tiles
+            ]
 
         own_keys = jnp.concatenate([pool[0, group, y, core, z, x], own_mask_ref[...]], axis=1)
         own_values = jnp.concatenate(
@@ -220,10 +253,7 @@
         )
         own_row = lax.broadcasted_iota(jnp.int32, (row_tile, rows), 0) % rows
         own_column = lax.broadcasted_iota(jnp.int32, (row_tile, rows), 1)
-        for tile in tiles:
-            scores = lax.dot_general(
-                query_s[tile, :], own_keys, contract, preferred_element_type=jnp.float32
-            )
+        for tile, scores in zip(tiles, logits(own_keys)):
             scores = jnp.where(own_column <= own_row, scores, MASKED)
             best = jnp.max(scores, axis=1, keepdims=True)
             weights = jnp.exp2((scores - best) * EXP2_SCALE).astype(jnp.bfloat16)
@@ -238,10 +268,7 @@
             values = jnp.concatenate(
                 [value_rows, jnp.ones((key_tile, HEAD_SIZE), jnp.bfloat16)], axis=1
             )
-            for tile in tiles:
-                scores = lax.dot_general(
-                    query_s[tile, :], keys, contract, preferred_element_type=jnp.float32
-                )
+            for tile, scores in zip(tiles, logits(keys)):
                 before = best_s[tile, :1]
                 best = jnp.maximum(before, jnp.max(scores, axis=1, keepdims=True))
                 factor = jnp.exp2((before - best) * EXP2_SCALE)
@@ -253,59 +280,62 @@
             return 0
 
         lax.fori_loop(0, steps, key_step, 0)
-        for local in range(GROUP):
+        for place, local in enumerate(locals_here):
             head = group * GROUP + local
-            tile = slice(local * rows, (local + 1) * rows)
+            tile = slice(place * rows, (place + 1) * rows)
             out_ref[:, head * HEAD_SIZE : (head + 1) * HEAD_SIZE] = (
                 acc_s[tile, :HEAD_SIZE] / acc_s[tile, HEAD_SIZE:]
             ).astype(jnp.bfloat16)
 
-    for part in range(4):
+    parts = KEY_VALUE_HEADS
+    for part in range(parts):
         stage_line(part)
+    build_masks()
+
+    def run(stage, part):
+        if part < parts:
+            stage(part)
+
     stage_first(0)
     stage_second(0)
     stage_first(1)
     stage_core(0)
+    stage_second(1)
+    stage_first(2)
     stage_done(0)
-    attend_group(0)
-    stage_first(2)
-    stage_second(1)
-    attend_group(1)
-    stage_first(3)
-    stage_core(1)
-    stage_second(2)
-    stage_done(1)
-    attend_group(2)
-    stage_second(3)
-    stage_core(2)
-    attend_group(3)
-    stage_core(3)
-    stage_done(2)
-    attend_group(4)
-    attend_group(5)
-    stage_done(3)
-    attend_group(6)
-    attend_group(7)
+    for part in range(parts):
+        attend_heads(part, range(GROUP // 2))
+        run(stage_core, part + 1)
+        run(stage_second, part + 2)
+        attend_heads(part, range(GROUP // 2, GROUP))
+        run(stage_first, part + 3)
+        run(stage_done, part + 1)
     for copy in copies.values():
         copy.wait_send()
 
 
-def fused(queries, keys, values, mask, own_mask, depth):
+def fused(queries, keys, values, vertical, slash, depth):
     rows = queries.shape[0]
-    parts = 4
-    tokens = mask.shape[0]
+    parts = KEY_VALUE_HEADS
+    tokens = rows * 8 * depth
+    blocks = rows // BLOCK
+    tables = [jnp.repeat(table.T, blocks, axis=1) for table in (vertical, slash)]
+    half = GROUP * rows // 2
     pairs = QUERY_HEADS * rows * tokens
     whole = pl.BlockSpec(memory_space=pltpu.VMEM)
     return pl.pallas_call(
-        functools.partial(fused_kernel, KEY_VALUE_HEADS // parts),
+        fused_kernel,
         out_shape=jax.ShapeDtypeStruct(queries.shape, jnp.bfloat16),
         in_specs=[whole] * 5,
         out_specs=whole,
         scratch_shapes=[
             pltpu.VMEM((2, KEY_VALUE_HEADS, 2, 2, depth, 2, rows, HEAD_SIZE), jnp.bfloat16),
-            pltpu.VMEM((GROUP * rows, 2 * HEAD_SIZE), jnp.bfloat16),
-            pltpu.VMEM((GROUP * rows, HEAD_SIZE), jnp.float32),
-            pltpu.VMEM((GROUP * rows, 2 * HEAD_SIZE), jnp.float32),
+            pltpu.VMEM((tokens, HEAD_SIZE), jnp.bfloat16),
+            pltpu.VMEM((rows, HEAD_SIZE), jnp.bfloat16),
+            pltpu.VMEM((tokens // BLOCK, HEAD_SIZE), jnp.float32),
+            pltpu.VMEM((half, 2 * HEAD_SIZE), jnp.bfloat16),
+            pltpu.VMEM((half, HEAD_SIZE), jnp.float32),
+            pltpu.VMEM((half, 2 * HEAD_SIZE), jnp.float32),
             pltpu.SemaphoreType.DMA((2, parts, depth + 2)),
             pltpu.SemaphoreType.DMA((2, parts, depth + 2)),
         ],
@@ -315,7 +345,7 @@
         cost_estimate=pl.CostEstimate(
             flops=pairs * HEAD_SIZE * 8, bytes_accessed=8 << 20, transcendentals=pairs
         ),
-    )(queries, keys, values, mask, own_mask)
+    )(queries, keys, values, *tables)
 
 
 def mask_columns(vertical, slash, first_block, blocks, block_total):
@@ -344,11 +374,12 @@
     total_bytes = 2 * tokens * keys.shape[1] * keys.dtype.itemsize
     tight = total_bytes > (32 << 20)
     heads = 1
+    staged = rows == 2 * BLOCK and lax.axis_size("rep") == 4 and lax.axis_size("seq") % 2 == 0
+    if staged and not tight:
+        return fused(queries, keys, values, vertical, slash, lax.axis_size("seq") // 2)
     mask, own_mask = mask_columns(
         vertical, slash, position * (rows // BLOCK), rows // BLOCK, tokens // BLOCK
     )
-    if not tight and lax.axis_size("rep") == 4 and lax.axis_size("seq") % 2 == 0:
-        return fused(queries, keys, values, mask, own_mask, lax.axis_size("seq") // 2)
     position = position.astype(jnp.int32).reshape(1)
     out = None
     for first in range(0, KEY_VALUE_HEADS, heads):

time: 144 us -> 119 us (0.83)
  Pallas kernels: 136 us -> 113 us
  other arithmetic: 2.16 us -> 0 us
    pallas_call x1, Pallas kernels: 136 us -> 113 us  [fused(): pl.pallas_call(fused_kernel, out_shape=jax.ShapeDtypeStruct(queries.shape...]
    reduce_or x2 -> x0, other arithmetic: 2.01 us -> none  [the longest x1 1.12 us: mask_columns(): jnp.any(slash[None, :, None, :] == gap[:, None, :, None], axis=-1)]
    broadcast_in_dim x2, local copies, waits for them, and re-layouts: 1.72 us -> 0.05 us  [fused(): jnp.repeat(table.T, blocks, axis=1)]
    transpose x0 -> x2, local copies, waits for them, and re-layouts: none -> 1.57 us  [fused(): tables = [jnp.repeat(table.T, blocks, axis=1) for table in (vertical, sla...]
where the time goes in v2:
time: 119 us
  Pallas kernels  113 us (95%)
  local copies, waits for them, and re-layouts  6.06 us (5%)
    pallas_call x1, Pallas kernels, fused(): pl.pallas_call(fused_kernel, out_shape=jax.ShapeDtypeStruct(queries.shape...  113 us
    unnamed x1, local copies, waits for them, and re-layouts  3.1 us

profile of v2, /device:TPU:13, one launch (start us, length us, event | category | flops | bytes accessed | tf_op | source)
XLA Modules:
  0.0 119.0 jit_solution(4934797195764922003)
XLA Ops:
  0.0 0.8 copy.6
  0.8 0.7 copy.8.column_ref
  1.5 0.8 copy.7
  2.3 0.7 copy.9.offset_ref
  3.0 113.0 %shard_map.55 = bf16[128,8192]{1,0:T(8,128)(2,1)} custom-call(bf16[128,8192]{1,0:T(8,128)(2,1)} %q_ref.1, bf16[128,1024]{1,0:T(8,128)(2,1)} %key_ref.1, bf16[128,1024]{1,0:T(8,128)(2,1)} %value_ref.1, s32[24,128]{1,0:T(8,128)} %copy.8.column_ref, s32[24,128]{1,0:T(8,128)} %copy.9.offset_ref), custom_call_target="tpu_custom_call" | custom-call | flops 34359738368 | bytes 8388608 | tf_op jit(solution)/shard_map/pallas_call | solution.py:326
  116.0 3.1 %copy.11 = bf16[128,8192]{1,0:T(8,128)(2,1)} copy(bf16[128,8192]{1,0:T(8,128)(2,1)} %shard_map.55) | data formatting | bytes 4194304
  (2 shorter events, 0.0 us)
